TPU v7x, 128 devices: a whole 4x4x4 slice. The times are simulated.
128 devices in a mesh: gx: 8 (over z, x_hi), gy: 4 (over x_lo, core), gz: 4 (over y).
Axes of the slice: x: 4 (x_hi: 2, x_lo: 2; x = x_hi * 2 + x_lo), y: 4, z: 4, core: 2. Of those that a mesh axis runs over, the one named last changes fastest.
Arguments:
- fixed_image: bfloat16 [256, 512, 1024], P('gz', 'gy', 'gx'), may hold values from -6 to 6
- moving_image: bfloat16 [256, 512, 1024], P('gz', 'gy', 'gx'), may hold values from -6 to 6
- block_shift: int32 [2, 4, 4, 8], P(None, 'gz', 'gy', 'gx'), may hold values from -1 to 0
- fraction: int32 [3, 4, 4, 8], P(None, 'gz', 'gy', 'gx'), may hold values from 0 to 63
- brick_valid: int32 [4, 4, 8], P('gz', 'gy', 'gx'), may hold values 0 or 1
- precond_x: float32 [64, 64], replicated, may hold values from -0.75 to 0.75
- precond_y: float32 [32, 32], replicated, may hold values from -1 to 1
- precond_z: float32 [16, 16], replicated, may hold values from -1.5 to 1.5
Outputs:
- gradient: float32 [3, 32, 64, 128], P(None, 'gz', 'gy', 'gx')
All inputs are finite; a program needn't handle non-finite values. No bound on the sum of `brick_valid` on one device may be relied on, other than what follows from the above.
Results may differ from a plain program's by a relative error of at most 0.00035.
Values may be sent and summed in bfloat16 or wider, within the bound.
A program may use at most 192 MiB of HBM per device.

v0:
```python
import jax
import jax.numpy as jnp
import numpy as np
from jax import lax
from jax.experimental import pallas as pl
from jax.experimental.pallas import tpu as pltpu
from jax.sharding import PartitionSpec as P

S = 8
SIDE = 128
DEPTH = 64
CELLS = DEPTH // S
HALF = S // 2
PIECES = 2 * CELLS
GX, GY, GZ = 8, 4, 4
FULL = lax.Precision.HIGHEST
F32 = jnp.float32
BF16 = jnp.bfloat16
MESH = pl.DeviceIdType.MESH


def tap_polynomials():
    j = np.arange(S, dtype=np.float64)
    basis = np.stack(
        [np.ones(S), j + 1, (j + 1) * (j + 2) / 2, (j + 1) * (j + 2) * (j + 3) / 6], axis=1
    )
    taps = []
    for a in range(4):
        u = np.abs(j / S - (a - 1))
        taps.append(
            np.where(u < 1, 2 / 3 - u**2 + u**3 / 2, np.where(u < 2, (2 - u) ** 3 / 6, 0.0))
        )
    return np.linalg.lstsq(basis, np.stack(taps, axis=1), rcond=None)[0]


TAPS = tap_polynomials()


def iota(shape, dim):
    return lax.broadcasted_iota(jnp.int32, shape, dim)


def spline(distance):
    dist = jnp.abs(distance)
    inner = 2.0 / 3.0 - dist * dist + dist * dist * dist / 2.0
    far = 2.0 - dist
    outer = far * far * far / 6.0
    return jnp.where(dist < 1.0, inner, jnp.where(dist < 2.0, outer, 0.0))


def weight(gap):
    gap = jnp.abs(gap)
    return jnp.where(gap == 0, 0.75, jnp.where(gap == 1, 0.5, jnp.where(gap == 2, 0.125, 0.0)))


def split(value):
    high = value.astype(BF16)
    return high, (value - high.astype(F32)).astype(BF16)


def mm(a, b):
    return jnp.dot(a, b, preferred_element_type=F32)


def mm_full(a, b, dims=((1,), (0,))):
    return lax.dot_general(a, b, (dims, ((), ())), precision=FULL, preferred_element_type=F32)


def kernel(
    mov, fix, shift_h, frac_h, valid_h, px_h, py_h, pz_h, out,
    shift, frac, valid, px, py, pz,
    own, relay, land, stage, sib1, sib2, fixed,
    flag_out, flag_in, e_own, e_x, e_up, e_up_x, e_down, e_down_x, t_sel, a_bot, b_bot,
    lhs, rhs, a_buf, b_buf, mom, rhs_x, lhs_y, acc, coarse, w_c,
    w_z, w_x, m_y, c_z, c_y, c_x, c_out, top_out, top_in, low_out, low_in, f_y, x_out, x_in, fold, h_x,
    local_sem, h1_s, h1_r, h2_s, h2_r, s1_s, s1_r, s2_s, s2_r,
    edge_s, edge_r, fine_s, fine_r, cz_s, cz_r, cy_s, cy_r, cx_s, cx_r,
):
    g, r, l = lax.axis_index("gx"), lax.axis_index("gy"), lax.axis_index("gz")
    across = lax.rem(r + 2, GY)
    sibling = (g, r + 1 - 2 * lax.rem(r, 2), l)
    partner = (g, across, l)

    def remote(src, dst, send, recv, device):
        return pltpu.make_async_remote_copy(
            src_ref=src, dst_ref=dst, send_sem=send, recv_sem=recv,
            device_id=device, device_id_type=MESH,
        )

    smalls = [
        pltpu.make_async_copy(src, dst, local_sem.at[2 + i])
        for i, (src, dst) in enumerate(
            ((shift_h, shift), (frac_h, frac), (valid_h, valid), (px_h, px), (py_h, py), (pz_h, pz))
        )
    ]
    for copy in smalls:
        copy.start()
    load_own = pltpu.make_async_copy(mov, own.at[pl.ds(0, DEPTH)], local_sem.at[0])
    load_fixed = pltpu.make_async_copy(fix, fixed, local_sem.at[1])
    load_own.start()
    load_fixed.start()

    peers = [(lax.rem(g + o, GX), r, l) for o in (1, 2, 4, 6, 7)]
    peers += [(g, lax.rem(r + o, GY), l) for o in range(1, GY)]
    peers += [(g, r, lax.rem(l + o, GZ)) for o in range(1, GZ)]
    peers += [(lax.rem(g + o, GX), across, l) for o in (1, GX - 1)]
    mate = g + 1 - 2 * lax.rem(g, 2)
    peers += [(mate, lax.rem(r + o, GY), l) for o in (1, 3)]
    barrier = pltpu.get_barrier_semaphore()
    for peer in peers:
        pl.semaphore_signal(barrier, inc=1, device_id=peer, device_id_type=MESH)
    for copy in smalls:
        copy.wait()
    ox, oy = shift[0], shift[1]
    tx = frac[0].astype(F32) / 64.0
    ty = frac[1].astype(F32) / 64.0
    tz = frac[2].astype(F32) / 64.0
    live = valid[0, 0, 0].astype(F32)
    flag_out[...] = jnp.full((8, SIDE), -oy.astype(F32), F32)
    pl.semaphore_wait(barrier, len(peers))

    def part(k, h):
        if isinstance(k, int):
            return pl.ds(k * S + h * HALF, HALF + (k == CELLS - 1 and h == 1)), 2 * k + h
        return pl.ds(pl.multiple_of(k * S + h * HALF, HALF), HALF), 2 * k + h

    def source(piece):
        return own if piece[0].size > HALF else mov

    def h1(piece, src=None):
        sl, i = piece
        if src is None:
            src = source(piece)
        return remote(
            src.at[sl], relay.at[sl], h1_s.at[i], h1_r.at[i], (lax.rem(g + 1, GX), across, l)
        )

    def h2(src, piece):
        sl, i = piece
        return remote(src.at[sl], land.at[sl], h2_s.at[i], h2_r.at[i], partner)

    def s1(piece):
        sl, i = piece
        return remote(source(piece).at[sl], sib1.at[sl], s1_s.at[i], s1_r.at[i], sibling)

    def s2(src, piece):
        sl, i = piece
        return remote(src.at[sl], sib2.at[sl], s2_s.at[i], s2_r.at[i], sibling)

    has_next, has_prev = g < GX - 1, g > 0
    above, below = l < GZ - 1, l > 0
    has_low, has_high = r > 0, r < GY - 1
    row0, row1, row2, row3 = (r == i for i in range(4))
    either = jnp.logical_or

    left = (lax.rem(g + GX - 1, GX), r, l)
    right = (lax.rem(g + 1, GX), r, l)
    low_row = (g, lax.rem(r + GY - 1, GY), l)
    high_row = (g, lax.rem(r + 1, GY), l)
    low_slab = (g, r, lax.rem(l + GZ - 1, GZ))
    high_slab = (g, r, lax.rem(l + 1, GZ))

    plane = remote(mov.at[pl.ds(0, 1)], own.at[pl.ds(DEPTH, 1)], edge_s.at[6], edge_r.at[6], low_slab)
    flag_up = remote(flag_out, flag_in, edge_s.at[7], edge_r.at[7], partner)
    flag_left = remote(flag_out, flag_in, edge_s.at[7], edge_r.at[7], left)
    asks_left = jnp.logical_and(row3, has_prev)
    asked = jnp.logical_and(row3, has_next)

    def early(k):
        @pl.when(jnp.logical_and(has_next, jnp.logical_not(row3)))
        def _():
            h1(part(k, 0)).start()

    early(7)

    @pl.when(below)
    def _():
        plane.start()

    @pl.when(row2)
    def _():
        flag_up.start()

    @pl.when(asks_left)
    def _():
        flag_left.start()

    @pl.when(jnp.logical_not(row3))
    def _():
        s1(part(7, 0)).start()
        s1(part(6, 0)).start()

    early(6)

    def blend(first, second, sl):
        flagged = jnp.max(flag_in[...]) > 0.5
        for j in range(sl.size):
            z = sl.start + j
            stage[z] = jnp.where(flagged, first[z], second[z])

    def send(piece):
        @pl.when(jnp.logical_and(has_next, jnp.logical_not(row3)))
        def _():
            h1(piece).start()

        @pl.when(row3)
        def _():
            s1(piece).wait_recv()

        @pl.when(asked)
        def _():
            blend(sib1, own, piece[0])
            h1(piece, stage).start()

    zero_plane = jnp.zeros((1, SIDE, SIDE), BF16)

    @pl.when(jnp.logical_not(above))
    def _():
        own[pl.ds(DEPTH, 1)] = zero_plane

    @pl.when(jnp.logical_not(has_prev))
    def _():
        def clear(z, carry):
            relay[pl.ds(z, 1)] = zero_plane
            return carry

        lax.fori_loop(0, DEPTH + 1, clear, 0)

    load_own.wait()

    @pl.when(asked)
    def _():
        flag_left.wait_recv()

    @pl.when(row3)
    def _():
        send(part(7, 0))
        send(part(6, 0))

    lane = iota((SIDE, SIDE), 1)
    row = iota((SIDE, SIDE), 0)

    def edge_step(z, carry):
        t, s = carry
        value = own[z].astype(F32)
        t = jnp.where(lane == z, jnp.broadcast_to(value[:, 0:1], (SIDE, SIDE)), t)
        s = jnp.where(row[:80] == z, jnp.broadcast_to(value[0:1, :], (80, SIDE)), s)
        return t, s

    t_own, s_own = lax.fori_loop(
        0, DEPTH, edge_step, (jnp.zeros((SIDE, SIDE), F32), jnp.zeros((80, SIDE), F32))
    )

    @pl.when(above)
    def _():
        plane.wait_recv()

    t_own, s_own = edge_step(DEPTH, (t_own, s_own))
    rows_s, rows_t = pl.ds(0, 80), pl.ds(80, 80)
    e_own[rows_s, :] = s_own.astype(BF16)
    e_own[rows_t, :] = jnp.transpose(t_own)[:80].astype(BF16)

    s_right = remote(e_own.at[rows_s], e_x.at[rows_s], edge_s.at[0], edge_r.at[0], right)
    t_left = remote(e_own.at[rows_t], e_x.at[rows_t], edge_s.at[1], edge_r.at[1], left)
    own_low = remote(e_own, e_up, edge_s.at[2], edge_r.at[2], low_row)
    x_low = remote(e_x, e_up_x, edge_s.at[3], edge_r.at[3], low_row)
    own_high = remote(e_own.at[rows_t], e_down, edge_s.at[4], edge_r.at[4], high_row)
    x_high = remote(e_x.at[rows_t], e_down_x, edge_s.at[5], edge_r.at[5], high_row)

    @pl.when(has_next)
    def _():
        s_right.start()

    @pl.when(has_prev)
    def _():
        t_left.start()

    @pl.when(has_low)
    def _():
        own_low.start()

    @pl.when(has_high)
    def _():
        own_high.start()

    @pl.when(jnp.logical_not(row3))
    def _():
        for k, h in ((7, 1), (6, 1), (5, 0), (5, 1)):
            s1(part(k, h)).start()

    send(part(7, 1))

    moved_x, moved_y = ox != 0, oy != 0
    both = jnp.logical_and(moved_x, moved_y)

    use_own = jnp.logical_not(jnp.logical_or(moved_x, moved_y))
    only_x = jnp.logical_and(moved_x, jnp.logical_not(moved_y))
    only_y = jnp.logical_and(moved_y, jnp.logical_not(moved_x))
    use_land = either(
        only_x, either(jnp.logical_and(row2, only_y), jnp.logical_and(row3, both))
    )
    use_sib1 = jnp.logical_and(either(row1, row3), only_y)
    use_sib2 = jnp.logical_and(either(row1, row2), both)

    def choose(z):
        value = jnp.where(use_sib2, sib2[z], jnp.zeros((SIDE, SIDE), BF16))
        value = jnp.where(use_sib1, sib1[z], value)
        value = jnp.where(use_land, land[z], value)
        return jnp.where(use_own, own[z], value)

    def forward(k, h):
        piece = part(k, h)

        @pl.when(has_prev)
        def _():
            h1(piece).wait_recv()

        @pl.when(row0)
        def _():
            s1(piece).wait_recv()
            blend(sib1, relay, piece[0])
            h2(stage, piece).start()

        @pl.when(jnp.logical_not(row0))
        def _():
            h2(relay, piece).start()

        @pl.when(row3)
        def _():
            s2(relay, piece).start()

        if isinstance(k, int) and k >= 6:
            send(part(*{(7, 0): (6, 1), (6, 0): (5, 0), (7, 1): (5, 1), (6, 1): (4, 0)}[k, h]))
        else:
            @pl.when(k >= 1 + h)
            def _():
                send(part(k - 1 - h, 1 - h))

    def landing(piece):
        h2(relay, piece).wait_recv()

        @pl.when(row0)
        def _():
            s2(land, piece).start()

        @pl.when(row1)
        def _():
            s1(piece).wait_recv()

        @pl.when(either(row1, row2))
        def _():
            s2(relay, piece).wait_recv()

    up_z = remote(top_out, top_in, fine_s.at[0], fine_r.at[0], high_slab)

    @pl.when(row0)
    def _():
        flag_up.wait_recv()

    forward(7, 0)

    rhs_lane = iota((2 * SIDE, 2 * SIDE), 1)
    rhs_row = iota((2 * SIDE, 2 * SIDE), 0)
    col = lax.rem(rhs_lane, SIDE)
    is_lerp = rhs_lane < SIDE
    here = jnp.where(is_lerp, 1.0 - tx, -1.0)
    there = jnp.where(is_lerp, tx, 1.0)
    top = jnp.where(rhs_row == col, here, jnp.where(rhs_row == col + 1, there, 0.0))
    rhs[...] = jnp.where(
        rhs_row < SIDE, top, jnp.where(col == SIDE - 1, there, 0.0)
    ).astype(BF16)

    point = lax.rem(lane, 32) - 8
    tap = lane // 32
    px_ok = jnp.logical_and(g * 16 + point >= 0, g * 16 + point < 16 * GX)
    basis_x = jnp.where(px_ok, spline(row.astype(F32) / S - point.astype(F32)), 0.0)
    for m in range(4):
        scale = jnp.full((SIDE, SIDE), float(TAPS[m, 3]), F32)
        for a in (2, 1, 0):
            scale = jnp.where(tap == a, float(TAPS[m, a]), scale)
        high, low = split(basis_x * scale)
        for half in range(2):
            rhs_x[pl.ds(m * 256 + half * 128, 128), pl.ds(0, 128)] = high
            rhs_x[pl.ds(m * 256 + half * 128, 128), pl.ds(128, 128)] = low

    q_point = iota((32, SIDE), 0) - 8
    q_ok = jnp.logical_and(r * 16 + q_point >= 0, r * 16 + q_point < 16 * GY)
    basis_y = jnp.where(
        q_ok, spline(iota((32, SIDE), 1).astype(F32) / S - q_point.astype(F32)), 0.0
    ) * (live * S ** (-1.5))
    high, low = split(basis_y)
    lhs_y[pl.ds(0, 32), pl.ds(0, 128)] = high
    lhs_y[pl.ds(0, 32), pl.ds(128, 128)] = high
    lhs_y[pl.ds(32, 32), pl.ds(0, 128)] = low
    lhs_y[pl.ds(32, 32), pl.ds(128, 128)] = jnp.zeros((32, SIDE), BF16)

    coarse_y = mm_full(weight(iota((16, 32), 1) - 8 - 2 * (iota((16, 32), 0) - 1)), basis_y)
    high, low = split(coarse_y)
    lhs_y[pl.ds(64, 16), pl.ds(0, 128)] = high
    lhs_y[pl.ds(64, 16), pl.ds(128, 128)] = high
    lhs_y[pl.ds(80, 16), pl.ds(0, 128)] = low
    lhs_y[pl.ds(80, 16), pl.ds(128, 128)] = jnp.zeros((16, SIDE), BF16)

    def cell_weights(k, carry):
        z_point = k + row // 32 - 1
        z_ok = jnp.logical_and(l * 8 + z_point >= 0, l * 8 + z_point < 8 * GZ)
        both_w = weight(z_point - 2 * (lane // 16 - 1)) * weight(
            lax.rem(row, 32) - 8 - 2 * (lax.rem(lane, 16) - 1)
        )
        w_c[k] = jnp.where(z_ok, both_w, 0.0).astype(BF16)
        return carry

    lax.fori_loop(0, CELLS, cell_weights, 0)
    coarse[...] = jnp.zeros((48, SIDE), F32)
    wr, wl = iota((512, SIDE), 0), iota((512, SIDE), 1)

    forward(6, 0)

    def arrive(copy, dst, ok):
        @pl.when(ok)
        def _():
            copy.wait_recv()

        @pl.when(jnp.logical_not(ok))
        def _():
            dst[...] = jnp.zeros(dst.shape, BF16)

    arrive(s_right, e_x.at[rows_s], has_prev)
    arrive(t_left, e_x.at[rows_t], has_next)

    @pl.when(has_low)
    def _():
        x_low.start()

    @pl.when(has_high)
    def _():
        x_high.start()

    kz = 4 * (iota((512, 16), 0) // 128) + lax.rem(iota((512, 16), 0) // 16, 8) - 1
    pick_z = (kz == iota((512, 16), 1)).astype(F32)
    spread_z = weight(l * 8 + iota((16, SIDE), 1) // 16 - 2 * iota((16, SIDE), 0))
    full_z = mm_full(mm_full(pick_z, pz[...], ((1,), (1,))), spread_z)
    full_z = jnp.where(lax.rem(wr, 16) == lax.rem(wl, 16), full_z, 0.0)
    high, low = split(full_z)
    w_z[0], w_z[1] = high, low

    jy = 8 * (iota((32, 64), 1) // 16) + lax.rem(iota((32, 64), 1), 16) - 1
    pick_y = (jy == iota((32, 64), 0)).astype(F32)
    spread_y = weight(r * 16 + iota((16, 32), 0) - 2 * iota((16, 32), 1))
    full_y = mm_full(spread_y, mm_full(py[...], pick_y))
    high, low = split(full_y)
    m_y[...] = jnp.concatenate(
        [
            jnp.concatenate([high.astype(F32), high.astype(F32)], axis=1),
            jnp.concatenate([low.astype(F32), jnp.zeros((16, 64), F32)], axis=1),
        ],
        axis=0,
    ).astype(BF16)

    xl = iota((64, 512), 1)
    spread_x = weight(16 * (2 * (xl // 128) + lax.rem(g, 2)) + lax.rem(xl, 16) - 2 * iota((64, 512), 0))
    kx = 8 * (g - lax.rem(g, 2) + iota((256, 64), 0) // 128) + lax.rem(iota((256, 64), 0), 16) - 1
    pick_x = (kx == iota((256, 64), 1)).astype(F32)
    full_x = mm_full(pick_x, mm_full(px[...], spread_x, ((0,), (0,))))
    same = lax.rem(iota((256, 512), 0) // 16, 8) == lax.rem(iota((256, 512), 1) // 16, 8)
    high, low = split(jnp.where(same, full_x, 0.0))
    w_x[0], w_x[1] = high, low

    def clear_acc(i, carry):
        acc[i] = jnp.zeros((32, 384), F32)
        return carry

    lax.fori_loop(0, 4, clear_acc, 0)

    arrive(own_low, e_up, has_high)
    arrive(own_high, e_down, has_low)
    arrive(x_low, e_up_x, has_high)
    arrive(x_high, e_down_x, has_low)

    def pick(stay, by_x, by_y, by_both):
        return jnp.where(moved_y, jnp.where(moved_x, by_both, by_y), jnp.where(moved_x, by_x, stay))

    def wide(ref, rows):
        return ref[rows, :].astype(F32)

    t_here, t_right = wide(e_own, rows_t), wide(e_x, rows_t)
    t_wide = pick(t_right, t_here, e_down_x[...].astype(F32), e_down[...].astype(F32))
    t_sel[...] = jnp.transpose(jnp.concatenate([t_wide, jnp.zeros((48, SIDE), F32)], axis=0))
    s_sel = pick(wide(e_up, rows_s), wide(e_up_x, rows_s), wide(e_own, rows_s), wide(e_x, rows_s))
    k_sel = pick(wide(e_up_x, rows_t), wide(e_up, rows_t), t_right, t_here)
    diag = jnp.where(lane[:80] == row[:80], jnp.broadcast_to(k_sel[:, 0:1], (80, SIDE)), 0.0)
    bottom = mm(jnp.concatenate([s_sel, diag], axis=1).astype(BF16), rhs[...])
    a_bot[...] = bottom[:, :SIDE]
    b_bot[...] = bottom[:, SIDE:]

    load_fixed.wait()

    def fill(z, j):
        lhs[pl.ds(j * SIDE, SIDE), pl.ds(0, SIDE)] = choose(z)
        lhs[pl.ds(j * SIDE, SIDE), pl.ds(SIDE, SIDE)] = jnp.where(lane == z, t_sel[...], 0.0).astype(BF16)

    def lerp_x(z, slot, count):
        for j in range(count):
            fill(z + j, j)
        both_x = mm(lhs[pl.ds(0, count * SIDE), :], rhs[...])
        for j in range(count):
            rows = slice(j * SIDE, (j + 1) * SIDE)
            a_buf[slot + j, pl.ds(0, SIDE), :] = both_x[rows, :SIDE]
            b_buf[slot + j, pl.ds(0, SIDE), :] = both_x[rows, SIDE:]
            a_buf[slot + j, pl.ds(SIDE, 1), :] = a_bot[pl.ds(z + j, 1), :]
            b_buf[slot + j, pl.ds(SIDE, 1), :] = b_bot[pl.ds(z + j, 1), :]

    def rows_of(j, y0):
        a = a_buf[j, pl.ds(y0, 16), :]
        b = b_buf[j, pl.ds(y0, 16), :]
        dy = a_buf[j, pl.ds(y0 + 1, 16), :] - a
        along_xy = a + ty * dy
        diff_xy = b + ty * (b_buf[j, pl.ds(y0 + 1, 16), :] - b)
        return along_xy, diff_xy, dy

    def compute(k):
        def tile(t, carry):
            y0 = pl.multiple_of(t * 16, 16)
            w1, x1, y1 = rows_of(S, y0)
            sums = [[jnp.zeros((16, SIDE), F32) for _ in range(4)] for _ in range(3)]
            for j in reversed(range(S)):
                w0, x0, yy0 = rows_of(j, y0)
                gz = w1 - w0
                res = w0 + tz * gz - fixed[k * S + j, pl.ds(y0, 16), :].astype(F32)
                grads = (x0 + tz * (x1 - x0), yy0 + tz * (y1 - yy0), gz)
                for d in range(3):
                    value = res * grads[d]
                    for m in range(4):
                        value = sums[d][m] + value
                        sums[d][m] = value
                w1, x1, y1 = w0, x0, yy0
            for d in range(3):
                for m in range(4):
                    high, low = split(sums[d][m])
                    place = pl.ds(pl.multiple_of(d * SIDE + y0, 16), 16)
                    mom[place, pl.ds(m * 256, 128)] = high
                    mom[place, pl.ds(m * 256 + 128, 128)] = low
            return carry

        lax.fori_loop(0, SIDE // 16, tile, 0)
        a_buf[S] = a_buf[0]
        b_buf[S] = b_buf[0]

        parts = mm(mom[...], rhs_x[...])
        parts = parts[:, :SIDE] + parts[:, SIDE:]
        wide = jnp.concatenate([parts[d * SIDE:(d + 1) * SIDE] for d in range(3)], axis=1)
        high, low = split(wide)
        h_x[pl.ds(0, SIDE), :] = high
        h_x[pl.ds(SIDE, SIDE), :] = low
        both_y = mm(lhs_y[...], h_x[...])
        rough = both_y[64:80] + both_y[80:96]
        rough = jnp.concatenate([rough[:, d * SIDE:(d + 1) * SIDE] for d in range(3)], axis=0)
        high, low = split(rough)
        weights = w_c[k]
        coarse[...] += mm(high, weights) + mm(low, weights)
        done = both_y[:32] + both_y[32:64]
        turn = lax.rem(k + 3, 4)
        base = (k + 3) // 4
        blocks = iota((32, SIDE), 1) // 32
        for d in range(3):
            moved = pltpu.roll(done[:, d * SIDE:(d + 1) * SIDE], turn * 32, 1)
            place = pl.ds(d * SIDE, SIDE)
            acc[base, :, place] += jnp.where(blocks >= turn, moved, 0.0)
            acc[base + 1, :, place] += jnp.where(blocks < turn, moved, 0.0)

    def land_half(k, h):
        piece = part(k, h)
        landing(piece)
        lerp_x(k * S + h * HALF, h * HALF, piece[0].size)

    def more(k):
        @pl.when(jnp.logical_not(row3))
        def _():
            for h in (0, 1):
                s1(part(k, h)).start()

    more(4)
    forward(7, 1)
    land_half(7, 0)
    forward(6, 1)
    land_half(7, 1)
    compute(7)

    def step(n, carry):
        k = 6 - n

        @pl.when(k >= 3)
        def _():
            more(k - 3)

        for h in (0, 1):
            @pl.when(k >= 1)
            def _(h=h):
                forward(k - 1, h)

            land_half(k, h)
        compute(k)

        @pl.when(k == 6)
        def _():
            top_out[...] = acc[3]

            @pl.when(above)
            def _():
                up_z.start()

        return carry

    lax.fori_loop(0, CELLS - 1, step, 0)

    c_z[l] = coarse[...]
    z_turns = (2, 1, 3)
    z_copies = [
        remote(c_z.at[l], c_z.at[l], cz_s.at[o], cz_r.at[l], (g, r, lax.rem(l + o, GZ))) for o in z_turns
    ]
    for copy in z_copies:
        copy.start()

    def drain(piece):
        h2(relay, piece).wait_send()

        @pl.when(jnp.logical_not(row3))
        def _():
            s1(piece).wait_send()

        @pl.when(has_next)
        def _():
            h1(piece).wait_send()

        @pl.when(either(row0, row3))
        def _():
            s2(relay, piece).wait_send()

    def drain_cell(k, carry):
        for h in (0, 1):
            drain(part(k, h))
        return carry

    lax.fori_loop(0, CELLS - 1, drain_cell, 0)
    drain_cell(CELLS - 1, 0)

    blocks = iota((32, SIDE), 1) // 32
    packed = jnp.zeros((32, SIDE), F32)
    for d in range(3):
        packed += jnp.where(
            blocks == d, pltpu.roll(acc[0, :, pl.ds(d * SIDE, SIDE)], 32 * (d + 1), 1), 0.0
        )
    low_out[...] = packed
    down_z = remote(low_out, low_in, fine_s.at[1], fine_r.at[1], low_slab)

    @pl.when(below)
    def _():
        down_z.start()

    fold[...] = acc[pl.ds(1, 2)]

    def weigh(block, weights, at):
        high, low = split(block)
        rows = block.shape[0]
        pair = mm(jnp.concatenate([high, low], axis=0), weights[0, at, :])
        return pair[:rows] + pair[rows:] + mm(high, weights[1, at, :])

    def span(dev):
        return pl.ds(pl.multiple_of(dev * SIDE, SIDE), SIDE)

    total = weigh(coarse[...], w_z, span(l))
    for o in (1, 3, 2):
        dev = lax.rem(l + o, GZ)
        remote(c_z.at[dev], c_z.at[dev], cz_s.at[o], cz_r.at[dev], partner).wait_recv()
        total += weigh(c_z[dev], w_z, span(dev))
    slot = GY * lax.rem(g, 2) + r
    c_y[slot] = total
    y_turns = [(1, 2), (1, 1), (1, 3), (1, 0), (0, 2), (0, 1), (0, 3)]
    y_copies = [
        remote(
            c_y.at[slot], c_y.at[slot], cy_s.at[i], cy_r.at[slot],
            (mate if dx else g, lax.rem(r + o, GY), l),
        )
        for i, (dx, o) in enumerate(y_turns)
    ]
    for copy in y_copies:
        copy.start()

    @pl.when(below)
    def _():
        up_z.wait_recv()
        fold[0] += top_in[...]

    @pl.when(above)
    def _():
        down_z.wait_recv()
        for d in range(3):
            turned = pltpu.roll(low_in[...], SIDE - 32 * (d + 1), 1)
            fold[1, :, pl.ds(d * SIDE, SIDE)] += jnp.where(blocks == 3, turned, 0.0)

    up_y = remote(fold.at[:, pl.ds(24, 8)], f_y.at[0], fine_s.at[2], fine_r.at[2], high_row)
    down_y = remote(fold.at[:, pl.ds(0, 8)], f_y.at[1], fine_s.at[3], fine_r.at[3], low_row)

    @pl.when(has_high)
    def _():
        up_y.start()

    @pl.when(has_low)
    def _():
        down_y.start()

    for i, (dx, o) in reversed(list(enumerate(y_turns))):
        dev = GY * lax.rem(g + dx, 2) + lax.rem(r + o, GY)
        remote(c_y.at[dev], c_y.at[dev], cy_s.at[i], cy_r.at[dev], partner).wait_recv()
    gathered = jnp.concatenate(
        [
            jnp.concatenate(
                [c_y[GY * dx + row, pl.ds(d * 16, 16), :] for dx in range(2) for d in range(3)], axis=1
            )
            for row in range(GY)
        ],
        axis=0,
    )
    high, low = split(gathered)
    both_y = mm(m_y[...], jnp.concatenate([high, low], axis=0))
    both_y = both_y[:16] + both_y[16:]
    both_y = jnp.concatenate(
        [
            jnp.concatenate(
                [both_y[:, (dx * 3 + d) * SIDE:(dx * 3 + d + 1) * SIDE] for dx in range(2)], axis=1
            )
            for d in range(3)
        ],
        axis=0,
    )
    corr = weigh(both_y, w_x, slice(None))
    for t in range(GZ):
        c_out[t] = corr[:, t * SIDE:(t + 1) * SIDE]

    z_own = g // 2
    x_copies = [
        remote(
            c_out.at[lax.rem(z_own + o, 4)], c_x.at[z_own], cx_s.at[o], cx_r.at[z_own],
            (lax.rem(g + 2 * o, GX), r, l),
        )
        for o in (2, 1, 3)
    ]
    for copy in x_copies:
        copy.start()

    @pl.when(has_low)
    def _():
        up_y.wait_recv()
        fold[:, pl.ds(8, 8), :] += f_y[0]

    @pl.when(has_high)
    def _():
        down_y.wait_recv()
        fold[:, pl.ds(16, 8), :] += f_y[1]

    spot = lax.rem(iota((16, SIDE), 1), 32)
    parts = [
        fold[half, pl.ds(8, 16), pl.ds(d * SIDE, SIDE)] for half in range(2) for d in range(3)
    ]
    to_right, to_left = jnp.zeros((16, SIDE), F32), jnp.zeros((16, SIDE), F32)
    for n, value in enumerate(parts):
        ends = jnp.where(jnp.logical_or(spot == 24, spot == 25), value, 0.0)
        to_right += ends if n == 0 else pltpu.roll(ends, 2 * n, 1)
        ends = jnp.where(spot == 7, value, 0.0)
        to_left += ends if n == 0 else pltpu.roll(ends, n, 1)
    x_out[0] = to_right
    x_out[1] = to_left
    up_x = remote(x_out.at[0], x_in.at[0], fine_s.at[4], fine_r.at[4], right)
    down_x = remote(x_out.at[1], x_in.at[1], fine_s.at[5], fine_r.at[5], left)

    @pl.when(has_next)
    def _():
        up_x.start()

    @pl.when(has_prev)
    def _():
        down_x.start()

    @pl.when(jnp.logical_not(has_prev))
    def _():
        x_in[0] = jnp.zeros((16, SIDE), F32)

    @pl.when(jnp.logical_not(has_next))
    def _():
        x_in[1] = jnp.zeros((16, SIDE), F32)

    corr = c_out[z_own]

    def take(o):
        dev = lax.rem(z_own + o, 4)
        remote(c_x.at[dev], c_x.at[dev], cx_s.at[o], cx_r.at[dev], partner).wait_recv()
        return c_x[dev]

    @pl.when(has_prev)
    def _():
        up_x.wait_recv()

    @pl.when(has_next)
    def _():
        down_x.wait_recv()

    from_left, from_right = x_in[0], x_in[1]
    fine = []
    for n, value in enumerate(parts):
        before = pltpu.roll(from_left, SIDE - 16 - 2 * n, 1)
        after = pltpu.roll(from_right, 16 - n, 1)
        value = value + jnp.where(jnp.logical_or(spot == 8, spot == 9), before, 0.0)
        fine.append(value + jnp.where(spot == 23, after, 0.0))

    for o in (1, 3, 2):
        corr += take(o)
    for half in range(2):
        for d in range(3):
            value = fine[half * 3 + d]
            for b in range(4):
                at = (half * 4 + b) * 16
                out[d, half * 4 + b] = (
                    value[:, b * 32 + 8:b * 32 + 24] + corr[d * 16:(d + 1) * 16, at:at + 16]
                )

    @pl.when(below)
    def _():
        plane.wait_send()
        down_z.wait_send()

    @pl.when(above)
    def _():
        up_z.wait_send()

    @pl.when(has_low)
    def _():
        own_low.wait_send()
        x_low.wait_send()
        down_y.wait_send()

    @pl.when(has_high)
    def _():
        own_high.wait_send()
        x_high.wait_send()
        up_y.wait_send()

    @pl.when(has_prev)
    def _():
        t_left.wait_send()
        down_x.wait_send()

    @pl.when(has_next)
    def _():
        s_right.wait_send()
        up_x.wait_send()

    @pl.when(row2)
    def _():
        flag_up.wait_send()

    @pl.when(asks_left)
    def _():
        flag_left.wait_send()

    for copy in z_copies + y_copies + x_copies:
        copy.wait_send()


def per_device(
    fixed_image, moving_image, block_shift, fraction, brick_valid, precond_x, precond_y, precond_z
):
    dma = pltpu.SemaphoreType.DMA
    vmem = pltpu.VMEM
    brick = vmem((DEPTH + 1, SIDE, SIDE), BF16)
    hbm_spec = pl.BlockSpec(memory_space=pltpu.HBM)
    smem = pltpu.SMEM
    vmem_spec = pl.BlockSpec(memory_space=pltpu.VMEM)
    return pl.pallas_call(
        kernel,
        out_shape=jax.ShapeDtypeStruct((3, 8, 16, 16), F32),
        in_specs=[hbm_spec] * 8,
        out_specs=vmem_spec,
        scratch_shapes=[
            smem((2,), jnp.int32), smem((3,), jnp.int32), smem((1, 1, 1), jnp.int32),
            vmem((64, 64), F32), vmem((32, 32), F32), vmem((16, 16), F32),
            brick, brick, brick, brick, brick, brick,
            vmem((DEPTH, SIDE, SIDE), BF16),
            vmem((8, SIDE), F32), vmem((8, SIDE), F32),
            vmem((160, SIDE), BF16), vmem((160, SIDE), BF16), vmem((160, SIDE), BF16),
            vmem((160, SIDE), BF16), vmem((80, SIDE), BF16), vmem((80, SIDE), BF16),
            vmem((SIDE, SIDE), F32), vmem((80, SIDE), F32), vmem((80, SIDE), F32),
            vmem((S * SIDE, 256), BF16), vmem((256, 256), BF16),
            vmem((S + 1, SIDE + 8, SIDE), F32), vmem((S + 1, SIDE + 8, SIDE), F32),
            vmem((3 * SIDE, 1024), BF16), vmem((1024, 256), BF16), vmem((96, 256), BF16),
            vmem((4, 32, 384), F32), vmem((48, SIDE), F32), vmem((CELLS, SIDE, SIDE), BF16),
            vmem((2, 512, SIDE), BF16), vmem((2, 256, 512), BF16), vmem((32, SIDE), BF16),
            vmem((GZ, 48, SIDE), F32), vmem((8, 48, SIDE), F32), vmem((4, 48, SIDE), F32), vmem((4, 48, SIDE), F32),
            vmem((32, 384), F32), vmem((32, 384), F32), vmem((32, SIDE), F32), vmem((32, SIDE), F32),
            vmem((2, 2, 8, 384), F32), vmem((2, 16, SIDE), F32), vmem((2, 16, SIDE), F32),
            vmem((2, 32, 384), F32), vmem((256, 384), BF16),
            dma((8,)),
            *[dma((PIECES,))] * 8,
            dma((8,)), dma((8,)), dma((6,)), dma((6,)),
            dma((GZ,)), dma((GZ,)), dma((8,)), dma((8,)), dma((4,)), dma((4,)),
        ],
        compiler_params=pltpu.CompilerParams(
            collective_id=0, has_side_effects=True, vmem_limit_bytes=53 * 2**20
        ),
        name="registration_gradient",
    )(
        *(
            pltpu.with_memory_space_constraint(x, pltpu.HBM)
            for x in (
                moving_image, fixed_image, block_shift.reshape(2), fraction.reshape(3)
            )
        ),
        brick_valid,
        *(pltpu.with_memory_space_constraint(x, pltpu.HBM) for x in (precond_x, precond_y, precond_z)),
    )


def solution(mesh):
    return jax.shard_map(
        per_device,
        mesh=mesh,
        in_specs=(
            P("gz", "gy", "gx"),
            P("gz", "gy", "gx"),
            P(None, "gz", "gy", "gx"),
            P(None, "gz", "gy", "gx"),
            P("gz", "gy", "gx"),
            P(),
            P(),
            P(),
        ),
        out_specs=P(None, "gz", "gy", "gx"),
        check_vma=False,
    )
```

profile of v0, /device:TPU:1, one launch (start us, length us, event | category | flops | bytes accessed | tf_op | source)
XLA Modules:
  0.0 82.3 jit_solution(7542442162611987568)
XLA Ops:
  0.7 81.0 %registration_gradient.1 = f32[3,8,16,16]{3,2,1,0:T(8,128)S(1)} custom-call(bf16[64,128,128]{2,1,0:T(8,128)(2,1)} %mov.1, bf16[64,128,128]{2,1,0:T(8,128)(2,1)} %fix.1, s32[2]{0:T(128)} %bitcast.2, s32[3]{0:T(128)} %bitcast.3, s32[1,1,1]{2,1,0:T(1,128)S(6)} %copy.10.valid_h, f32[64,64]{1,0:T(8,128)} %px_h.1, f32[32,32]{1,0:T(8,128)} %py_h.1, f32[16,16]{1,0:T(8,128)} %pz_h.1), custom_call_target="tpu_custom_call" | custom-call | tf_op jit(solution)/shard_map/registration_gradient/pallas_call | solution.py:878
  81.6 0.7 copy.11
where the time goes:
time: 82.4 us; the launch traced here: 82.3 us
  Pallas kernels  81 us (98%)
    pallas_call x1, Pallas kernels, per_device(): pl.pallas_call(kernel, out_shape=jax.ShapeDtypeStruct((3, 8, 16, 16), F32...  81 us

commit v1 on v0

--- a/solution.py
+++ b/solution.py
@@ -87,6 +87,15 @@
             device_id=device, device_id_type=MESH,
         )
 
+    peers = [(lax.rem(g + o, GX), r, l) for o in (1, 2, 4, 6, 7)]
+    peers += [(g, lax.rem(r + o, GY), l) for o in range(1, GY)]
+    peers += [(g, r, lax.rem(l + o, GZ)) for o in range(1, GZ)]
+    peers += [(lax.rem(g + o, GX), across, l) for o in (1, GX - 1)]
+    mate = g + 1 - 2 * lax.rem(g, 2)
+    peers += [(mate, lax.rem(r + o, GY), l) for o in (1, 3)]
+    barrier = pltpu.get_barrier_semaphore()
+    for peer in peers:
+        pl.semaphore_signal(barrier, inc=1, device_id=peer, device_id_type=MESH)
     smalls = [
         pltpu.make_async_copy(src, dst, local_sem.at[2 + i])
         for i, (src, dst) in enumerate(
@@ -100,15 +109,6 @@
     load_own.start()
     load_fixed.start()
 
-    peers = [(lax.rem(g + o, GX), r, l) for o in (1, 2, 4, 6, 7)]
-    peers += [(g, lax.rem(r + o, GY), l) for o in range(1, GY)]
-    peers += [(g, r, lax.rem(l + o, GZ)) for o in range(1, GZ)]
-    peers += [(lax.rem(g + o, GX), across, l) for o in (1, GX - 1)]
-    mate = g + 1 - 2 * lax.rem(g, 2)
-    peers += [(mate, lax.rem(r + o, GY), l) for o in (1, 3)]
-    barrier = pltpu.get_barrier_semaphore()
-    for peer in peers:
-        pl.semaphore_signal(barrier, inc=1, device_id=peer, device_id_type=MESH)
     for copy in smalls:
         copy.wait()
     ox, oy = shift[0], shift[1]

time: 82.4 us -> 82.4 us (level)
  no operation moved by 1% of the time
where the time goes in v1:
time: 82.4 us; the launch traced here: 82.3 us
  Pallas kernels  81 us (98%)
    pallas_call x1, Pallas kernels, per_device(): pl.pallas_call(kernel, out_shape=jax.ShapeDtypeStruct((3, 8, 16, 16), F32...  81 us

profile of v1, /device:TPU:1, one launch (start us, length us, event | category | flops | bytes accessed | tf_op | source)
XLA Modules:
  0.0 82.3 jit_solution(17556517255567419032)
XLA Ops:
  0.7 81.0 %registration_gradient.1 = f32[3,8,16,16]{3,2,1,0:T(8,128)S(1)} custom-call(bf16[64,128,128]{2,1,0:T(8,128)(2,1)} %mov.1, bf16[64,128,128]{2,1,0:T(8,128)(2,1)} %fix.1, s32[2]{0:T(128)} %bitcast.2, s32[3]{0:T(128)} %bitcast.3, s32[1,1,1]{2,1,0:T(1,128)S(6)} %copy.10.valid_h, f32[64,64]{1,0:T(8,128)} %px_h.1, f32[32,32]{1,0:T(8,128)} %py_h.1, f32[16,16]{1,0:T(8,128)} %pz_h.1), custom_call_target="tpu_custom_call" | custom-call | tf_op jit(solution)/shard_map/registration_gradient/pallas_call | solution.py:878
  81.6 0.7 copy.11
